TPU v7x, 512 devices: a whole 4x8x8 slice. The times are simulated.
512 devices in a mesh: row: 64 (over y, x, core), col: 8 (over z).
Axes of the slice: x: 4, y: 8, z: 8, core: 2. Of those that a mesh axis runs over, the one named last changes fastest.
Arguments:
- matrix: bfloat16 [4, 16384, 1, 2048], P(None, 'row', None, 'col'), may hold values from -0.045 to 2.375, as said below
Outputs:
- factored: float32 [4, 16384, 1, 2048], P(None, 'row', None, 'col')
Inputs may be any that keep to these rules, and one draw needn't show every extreme that they name: Only entries on or below the diagonal are read. The symmetric matrix built from the lower triangle has its leading 2 * 256 principal block positive definite.
All inputs are finite; a program needn't handle non-finite values.
Results may differ from a plain program's by a relative error of at most 0.0003.
Values sent between devices are 32-bit elements; how exact they have to be, the bound alone decides.
A program may use at most 64 MiB of HBM per device.

v0:
```python
import jax
import jax.numpy as jnp
from jax import lax
from jax.sharding import PartitionSpec as P

HIGH = lax.Precision.HIGHEST


def spread(value, axis, source):
    kept = jnp.where(lax.axis_index(axis) == source, value, 0).astype(value.dtype)
    return lax.psum(kept, axis)


def update_range(working, panel_rows, panel_cols, section, col_blocks, start_col, stop_col):
    product = jnp.einsum("rab,ldb->rald", panel_rows, panel_cols, precision=HIGH)
    active = (col_blocks > section)[None, None, :, None]
    return working.at[:, :, start_col:stop_col, :].add(
        jnp.where(active, -product, jnp.float32(0.0))
    )


def per_device(matrix):
    row_count = lax.axis_size("row")
    col_count = lax.axis_size("col")
    row_index = lax.axis_index("row")
    col_index = lax.axis_index("col")
    row_tiles, block, col_tiles, _ = matrix.shape
    working = matrix.astype(jnp.float32)
    identity = jnp.eye(block, dtype=jnp.float32)
    row_blocks = jnp.arange(row_tiles, dtype=jnp.int32) * row_count + row_index
    col_blocks = jnp.arange(col_tiles, dtype=jnp.int32) * col_count + col_index
    for section in range(2):
        root_row = section % row_count
        root_col = section % col_count
        diag_tile = working[section // row_count, :, section // col_count, :]
        diag_block = spread(diag_tile, "row", root_row)
        symmetric = jnp.tril(diag_block) + jnp.tril(diag_block, -1).T
        lower = jnp.linalg.cholesky(symmetric)
        inverse = jax.scipy.linalg.solve_triangular(lower, identity, lower=True)
        column = working[:, :, section // col_count, :]
        panel = jnp.einsum("rab,cb->rac", column, inverse, precision=HIGH)
        block_ids = row_blocks[:, None, None]
        own_panel = jnp.where(
            block_ids > section,
            panel,
            jnp.where(block_ids == section, lower[None], jnp.float32(0.0)),
        )
        panel_rows = spread(own_panel, "col", root_col)
        global_id = 0 + col_index
        source = global_id % row_count
        slot_index = global_id // row_count
        wanted = lax.dynamic_index_in_dim(panel_rows, slot_index, 0, keepdims=False)
        fetched = [spread(wanted, "row", source)]
        panel_cols = jnp.stack(fetched)
        panel_rows, panel_cols = (panel_rows, panel_cols)
        panel_slot = section // col_count
        current = working[:, :, panel_slot, :]
        working = working.at[:, :, panel_slot, :].set(
            jnp.where(col_index == section % col_count, panel_rows, current)
        )
        working = update_range(working, panel_rows, panel_cols, section, col_blocks, 0, col_tiles)
    global_rows = (
        (jnp.arange(row_tiles, dtype=jnp.int32) * row_count * block)[:, None]
        + row_index * block
        + jnp.arange(block, dtype=jnp.int32)[None, :]
    )
    global_cols = (
        (jnp.arange(col_tiles, dtype=jnp.int32) * col_count * block)[:, None]
        + col_index * block
        + jnp.arange(block, dtype=jnp.int32)[None, :]
    )
    keeper = global_rows[:, :, None, None] >= global_cols[None, None, :, :]
    return jnp.where(keeper, working, jnp.float32(0.0))


def solution(mesh):
    return jax.shard_map(
        per_device,
        mesh=mesh,
        in_specs=(P(None, "row", None, "col"),),
        out_specs=P(None, "row", None, "col"),
        check_vma=False,
    )
```

profile of v0, /device:TPU:1, one launch (start us, length us, event | category | flops | bytes accessed | tf_op | source)
XLA Modules:
  0.0 1068.4 jit_solution(239354329881305798)
XLA Ops:
  8.5 194.3 %all-reduce.8.cloned.1.call-done = f32[256,256]{1,0:T(8,128)} async-done(((f32[256,256]{1,0:T(8,128)}), f32[256,256]{1,0:T(8,128)}) %all-reduce.8.cloned.1.call-update) | async-done | bytes 262160 | tf_op jit(solution)/shard_map/psum | solution.py:11
  204.3 11.7 %cholesky.130 = f32[128,128]{1,0:T(8,128)S(1)} custom-call(f32[128,128]{1,0:T(8,128)S(1)} %cholesky.194), custom_call_target="Cholesky" | custom-call | tf_op jit(solution)/shard_map/jit(cholesky)/cholesky | solution.py:38
  216.1 9.8 custom-call.13
  226.4 11.7 %cholesky.147 = f32[128,128]{1,0:T(8,128)S(1)} custom-call(f32[128,128]{1,0:T(8,128)S(1)} %convolution_subtract_fusion.3), custom_call_target="Cholesky" | custom-call | tf_op jit(solution)/shard_map/jit(cholesky)/cholesky | solution.py:38
  240.4 4.3 while.10
  241.2 1.4 bitcast_dynamic-update-slice_fusion.4
  244.7 19.7 %custom-call.14 = f32[2,128,128]{1,2,0:T(8,128)S(1)} custom-call(f32[2,128,128]{2,1,0:T(8,128)S(1)} %get-tuple-element.85), custom_call_target="InvertDiagBlocksLowerTriangular" | custom-call | tf_op jit(solution)/shard_map/jit(_solve_triangular)/triangular_solve | solution.py:39
  265.4 1.6 fusion.4
  267.1 76.1 %all-reduce.10.cloned.1.call-done = f32[4,256,256]{2,1,0:T(8,128)} async-done(((f32[4,256,256]{2,1,0:T(8,128)}), f32[4,256,256]{2,1,0:T(8,128)}) %all-reduce.10.cloned.1.call-update) | async-done | bytes 1048592 | tf_op jit(solution)/shard_map/psum | solution.py:11
  343.1 1.7 select_bitcast_fusion.1
  344.9 190.3 %all-reduce.12.cloned.1.call-done = f32[256,256]{1,0:T(8,128)} async-done(((f32[256,256]{1,0:T(8,128)}), f32[256,256]{1,0:T(8,128)}) %all-reduce.12.cloned.1.call-update) | async-done | bytes 262160 | tf_op jit(solution)/shard_map/psum | solution.py:11
  535.2 2.7 fusion.5
  538.9 184.0 %all-reduce.14.cloned.1.call-done = f32[256,256]{1,0:T(8,128)} async-done(((f32[256,256]{1,0:T(8,128)}), f32[256,256]{1,0:T(8,128)}) %all-reduce.14.cloned.1.call-update) | async-done | bytes 262160 | tf_op jit(solution)/shard_map/psum | solution.py:11
  725.1 11.7 %cholesky.164 = f32[128,128]{1,0:T(8,128)S(1)} custom-call(f32[128,128]{1,0:T(8,128)S(1)} %cholesky.197), custom_call_target="Cholesky" | custom-call | tf_op jit(solution)/shard_map/jit(cholesky)/cholesky | solution.py:38
  736.9 9.8 custom-call.15
  747.2 11.7 %cholesky.181 = f32[128,128]{1,0:T(8,128)S(1)} custom-call(f32[128,128]{1,0:T(8,128)S(1)} %convolution_subtract_fusion.2), custom_call_target="Cholesky" | custom-call | tf_op jit(solution)/shard_map/jit(cholesky)/cholesky | solution.py:38
  761.7 4.3 while.11
  766.0 19.7 %custom-call.16 = f32[2,128,128]{1,2,0:T(8,128)S(1)} custom-call(f32[2,128,128]{2,1,0:T(8,128)S(1)} %get-tuple-element.86), custom_call_target="InvertDiagBlocksLowerTriangular" | custom-call | tf_op jit(solution)/shard_map/jit(_solve_triangular)/triangular_solve | solution.py:39
  786.6 2.0 fusion
  788.7 76.1 %all-reduce.16.cloned.1.call-done = f32[4,256,256]{2,1,0:T(8,128)} async-done(((f32[4,256,256]{2,1,0:T(8,128)}), f32[4,256,256]{2,1,0:T(8,128)}) %all-reduce.16.cloned.1.call-update) | async-done | bytes 1048592 | tf_op jit(solution)/shard_map/psum | solution.py:11
  864.8 1.7 select_bitcast_fusion
  866.6 190.2 %all-reduce.18.cloned.1.call-done = f32[256,256]{1,0:T(8,128)} async-done(((f32[256,256]{1,0:T(8,128)}), f32[256,256]{1,0:T(8,128)}) %all-reduce.18.cloned.1.call-update) | async-done | bytes 262160 | tf_op jit(solution)/shard_map/psum | solution.py:11
  1056.8 2.8 fusion.8
  1059.5 2.0 copy.10
  (77 shorter events, 18.7 us)
Async XLA Ops:
  6.5 196.3 %all-reduce.8.cloned.1.call-start = ((), (), s32[]{:S(2)}) async-start(), calls=%async_computation | async-start | bytes 524288 | tf_op jit(solution)/shard_map/psum | solution.py:11
  8.4 334.7 %all-reduce.10.cloned.1.call-start = ((), (), s32[]{:S(2)}) async-start(), calls=%async_computation.1 | async-start | bytes 2097152 | tf_op jit(solution)/shard_map/psum | solution.py:11
  202.9 1.2 copy-start.1
  264.3 1.0 copy-start
  267.0 268.2 %all-reduce.12.cloned.1.call-start = ((), (), s32[]{:S(2)}) async-start(), calls=%async_computation.2 | async-start | bytes 524288 | tf_op jit(solution)/shard_map/psum | solution.py:11
  344.8 378.1 %all-reduce.14.cloned.1.call-start = ((), (), s32[]{:S(2)}) async-start(), calls=%async_computation.3 | async-start | bytes 524288 | tf_op jit(solution)/shard_map/psum | solution.py:11
  538.6 326.2 %all-reduce.16.cloned.1.call-start = ((), (), s32[]{:S(2)}) async-start(), calls=%async_computation.4 | async-start | bytes 2097152 | tf_op jit(solution)/shard_map/psum | solution.py:11
  723.9 1.0 copy-start.2
  788.7 268.1 %all-reduce.18.cloned.1.call-start = ((), (), s32[]{:S(2)}) async-start(), calls=%async_computation.5 | async-start | bytes 524288 | tf_op jit(solution)/shard_map/psum | solution.py:11
Sparse Core Ops, SparseCore 0:
  10.8 191.9 all-reduce.7
  267.1 75.9 all-reduce.9
  347.0 188.1 all-reduce.11
  538.8 184.0 all-reduce.13
  788.8 75.9 all-reduce.15
  868.6 188.1 all-reduce.17
where the time goes:
time: 1070 us
  waiting for transfers between devices  911 us (85%)
  other arithmetic  115 us (11%)
  between operations  16.6 us (2%)
  local copies, waits for them, and re-layouts  13 us (1%)
  matrix products  11.7 us (1%)
    psum x6, waiting for transfers between devices, spread(): return lax.psum(kept, axis)  911 us
    another operation x13, other arithmetic, per_device(): lower = jnp.linalg.cholesky(symmetric)  68.7 us
    another operation x5, other arithmetic, per_device(): inverse = jax.scipy.linalg.solve_triangular(lower, identity, lower=True)  39.4 us
  transfers between devices with their start and end apart: 6, of which 6 were waited for; matrix products, arithmetic and copies ran while one was open for 0% of the time, Pallas kernels for 0%

commit v1 on v0

v1 whole, which is shorter than its diff:
```python
import jax
import jax.numpy as jnp
from jax import lax
from jax.experimental import pallas as pl
from jax.experimental.pallas import tpu as pltpu
from jax.sharding import PartitionSpec as P

MESH = pl.DeviceIdType.MESH
F32 = jnp.float32
NB = 256
STEP = 32
XS, YS, ZS = 4, 8, 8
R = 32
SKEW = 3
PER = 128 // R
CHUNKS = 4 * PER
PIECE = NB // YS
INV0, P10, INV1, AJ0, AJ1 = range(5)


def split3(x):
    h = x.astype(jnp.bfloat16)
    r = x - h.astype(F32)
    m = r.astype(jnp.bfloat16)
    return h, m, (r - m.astype(F32)).astype(jnp.bfloat16)


def mm_nt(a, b):
    return lax.dot_general(a, b, (((1,), (1,)), ((), ())), precision=lax.Precision.HIGHEST, preferred_element_type=F32)


def mm_nn(a, b):
    return lax.dot_general(a, b, (((1,), (0,)), ((), ())), precision=lax.Precision.HIGHEST, preferred_element_type=F32)


def iota(shape, d):
    return lax.broadcasted_iota(jnp.int32, shape, d)


def symmetric(x):
    keep = iota((NB, NB), 0) >= iota((NB, NB), 1)
    return jnp.where(keep, x, x.T)


def factor_start(W, a):
    W[:, 0:NB] = a
    W[:, NB:2 * NB] = jnp.where(iota((NB, NB), 0) == iota((NB, NB), 1), 1.0, 0.0).astype(F32)


def factor_step(W, k):
    base = pl.multiple_of(STEP * k, STEP)
    ra = W[pl.ds(base, STEP), 0:NB]
    rm = W[pl.ds(base, STEP), NB:2 * NB]
    ra = pltpu.roll(ra, lax.rem(NB - STEP * k, NB), 1)
    G = [[ra[8 * g:8 * g + 8, 0:128], ra[8 * g:8 * g + 8, 128:256],
          rm[8 * g:8 * g + 8, 0:128], rm[8 * g:8 * g + 8, 128:256]] for g in range(4)]
    full = (8, 128)
    sub = iota(full, 0)
    for t in range(4):
        cols = {g: [jnp.broadcast_to(G[g][0][:, 8 * t + i:8 * t + i + 1], full) for i in range(8)] for g in range(t, 4)}
        s = {(i, j): jnp.broadcast_to(cols[t][j][i:i + 1, :], full) for j in range(8) for i in range(j, 8)}
        row = [[jnp.broadcast_to(G[t][v][i:i + 1, :], full) for v in range(4)] for i in range(8)]
        for j in range(8):
            r = lax.rsqrt(s[j, j])
            for i in range(j + 1, 8):
                s[i, j] = s[i, j] * r
            for i2 in range(j + 1, 8):
                for i in range(i2, 8):
                    s[i, i2] = s[i, i2] - s[i, j] * s[i2, j]
            row[j] = [x * r for x in row[j]]
            for i in range(j + 1, 8):
                row[i] = [x - s[i, j] * y for x, y in zip(row[i], row[j])]
            for g in range(t + 1, 4):
                cols[g][j] = cols[g][j] * r
                for i in range(j + 1, 8):
                    cols[g][i] = cols[g][i] - s[i, j] * cols[g][j]
        for g in range(t + 1, 4):
            for v in range(4):
                p = [cols[g][j] * row[j][v] for j in range(8)]
                while len(p) > 1:
                    p = [a + b for a, b in zip(p[::2], p[1::2])]
                G[g][v] = G[g][v] - p[0]
        for v in range(4):
            x = row[0][v]
            for i in range(1, 8):
                x = jnp.where(sub == i, row[i][v], x)
            G[t][v] = x
    ua = jnp.concatenate([jnp.concatenate([G[g][0], G[g][1]], 1) for g in range(4)], 0)
    um = jnp.concatenate([jnp.concatenate([G[g][2], G[g][3]], 1) for g in range(4)], 0)
    ua = pltpu.roll(ua, STEP * k, 1)
    lhs = jnp.where(iota((STEP, NB), 1) >= STEP * (k + 1), ua, 0.0)
    W[pl.ds(base, STEP), 0:NB] = ua
    W[pl.ds(base, STEP), NB:2 * NB] = um
    a, b, c = split3(lhs)
    ah, am, al = split3(ua)
    mh, mm, ml = split3(um)
    left = jnp.concatenate([a, a, b, a, c, b], 0)
    dn = (((0,), (0,)), ((), ()))
    for lo, (h, m, l) in ((0, (ah, am, al)), (NB, (mh, mm, ml))):
        right = jnp.concatenate([h, m, h, l, h, m], 0)
        W[:, lo:lo + NB] = W[:, lo:lo + NB] - lax.dot_general(left, right, dn, preferred_element_type=F32)


def kernel(a_ref, o_ref, x0, x1, D, E, W, zsend, zrecv, bsend, brecv, ssend, srecv, esend, erecv):
    row = lax.axis_index("row")
    z = lax.axis_index("col")
    core = lax.rem(row, 2)
    x = lax.rem(row // 2, XS)
    y = row // (2 * XS)

    def at(x_, y_, z_, c_):
        return ((y_ * XS + x_) * 2 + c_, z_)

    is_src = (row == 0) & (z == 0)
    is_a11 = (row == 1) & (z == 1)
    is_a10 = (row == 1) & (z == 0)

    barrier = pltpu.get_barrier_semaphore()
    for d in range(1, ZS):
        pl.semaphore_signal(barrier, inc=1, device_id=at(x, y, lax.rem(z + d, ZS), core), device_id_type=MESH)
    for d in range(1, YS):
        pl.semaphore_signal(barrier, inc=1, device_id=at(x, lax.rem(y + d, YS), z, core), device_id_type=MESH)
    for d in range(1, XS):
        pl.semaphore_signal(barrier, inc=1, device_id=at(lax.rem(x + d, XS), y, z, core), device_id_type=MESH)
    pl.semaphore_signal(barrier, inc=1, device_id=at(x, y, z, 1 - core), device_id_type=MESH)

    @pl.when(is_src)
    def _():
        pl.semaphore_signal(barrier, inc=1, device_id=(1, 1), device_id_type=MESH)

    @pl.when(is_a11)
    def _():
        pl.semaphore_signal(barrier, inc=1, device_id=(0, 0), device_id_type=MESH)

    @pl.when(z == 0)
    def _():
        for s in range(4):
            x0[s] = a_ref[s].astype(F32)

        @pl.when(row == 0)
        def _():
            x0[0] = symmetric(x0[0])

    @pl.when(z == 1)
    def _():
        for s in range(4):
            x1[s] = a_ref[s].astype(F32)

        @pl.when(row == 1)
        def _():
            x1[0] = symmetric(x1[0])

    @pl.when(is_src)
    def _():
        factor_start(W, x0[0])

    pl.semaphore_wait(barrier, ZS + YS + XS - 2 + jnp.where(is_src | is_a11, 1, 0))

    def send_a10():
        return pltpu.make_async_remote_copy(src_ref=x0.at[0], dst_ref=E.at[0], send_sem=esend.at[0], recv_sem=erecv.at[0],
                                            device_id=(0, 0), device_id_type=MESH)

    def send_a11():
        return pltpu.make_async_remote_copy(src_ref=x1.at[0], dst_ref=E.at[1], send_sem=esend.at[0], recv_sem=erecv.at[1],
                                            device_id=(0, 0), device_id_type=MESH)

    @pl.when(is_a10)
    def _():
        send_a10().start()

    @pl.when(is_a11)
    def _():
        send_a11().start()

    zp = lax.rem(z + 1, ZS)
    zm = lax.rem(z + ZS - 1, ZS)
    hops = (z, lax.rem(ZS - z, ZS), lax.rem(z + ZS - 1, ZS), lax.rem(ZS + 1 - z, ZS))
    last = (ZS - 1, 1, ZS - 1, 2)

    def zcopy(st, c):
        buf = x0 if st < 2 else x1
        off = pl.multiple_of((0 if st % 2 == 0 else 128) + lax.rem(c, PER) * R, R)
        ref = buf.at[c // PER, pl.ds(off, R), :]
        return pltpu.make_async_remote_copy(src_ref=ref, dst_ref=ref, send_sem=zsend.at[st, c], recv_sem=zrecv.at[st, c],
                                            device_id=(row, zp if st % 2 == 0 else zm), device_id_type=MESH)

    def zreceives(st):
        return (hops[st] > 0) & (z != 0) if st == 2 else hops[st] > 0

    def zsends(st):
        return (z != last[st]) & (z != 0) if st == 2 else z != last[st]

    def ztick(n):
        for st in range(4):
            c = n - hops[st] * SKEW
            ok = (c >= 0) & (c < CHUNKS)

            @pl.when(ok & zreceives(st))
            def _():
                zcopy(st, c).wait_recv()

            @pl.when(ok & zsends(st))
            def _():
                zcopy(st, c).start()

    def root(b):
        if b < AJ0:
            return 0, 0, 0
        return z // 2, z, lax.rem(z, 2)

    def has(b):
        return z >= (0 if b == INV0 else 1 if b < AJ0 else 2)

    def piece(b, q, dest, sem):
        ref = D.at[b, pl.ds(pl.multiple_of(q * PIECE, PIECE), PIECE), :]
        return pltpu.make_async_remote_copy(src_ref=ref, dst_ref=ref, send_sem=bsend.at[b, sem], recv_sem=brecv.at[b, q],
                                            device_id=dest, device_id_type=MESH)

    def on_root(b):
        xr, zr, cr = root(b)
        return (x == xr) & (y == 0) & (z == zr) & (core == cr)

    def scatter(b, act):
        for d in range(1, YS):
            act(piece(b, d, at(x, d, z, core), d - 1))

    def send_x(b, act):
        for d in range(1, XS):
            act(piece(b, y, at(lax.rem(x + d, XS), y, z, core), 6 + d))

    def send_z(b, act):
        for d in range(1, ZS):
            act(piece(b, y, at(x, y, d, core), 9 + d))

    def send_y(b, act):
        xr, zr, _ = root(b)
        for d in range(1, YS):
            to = lax.rem(y + d, YS)

            @pl.when(jnp.logical_not((to == 0) & (x == xr) & (z == zr)))
            def _():
                act(piece(b, y, at(x, to, z, core), 16 + d))

    def start(cp):
        cp.start()

    def finish(cp):
        cp.wait_send()

    def relay_roles(b):
        xr, zr, cr = root(b)
        on_core = core == cr
        first = on_core & (x == xr) & (z == zr)
        second = on_core & (z == zr) if b < AJ0 else None
        third = on_core & has(b)
        return first, second, third

    def relay_sends(b, act):
        first, second, third = relay_roles(b)

        @pl.when(first & (z >= (2 if b >= AJ0 else 0)))
        def _():
            send_x(b, act)

        if second is not None:
            @pl.when(second)
            def _():
                send_z(b, act)

        @pl.when(third)
        def _():
            send_y(b, act)

    def relay(b):
        xr, zr, cr = root(b)
        takes = (core == cr) & (has(b) | (z == zr)) if b < AJ0 else (core == cr) & has(b)

        @pl.when(takes & jnp.logical_not(on_root(b)))
        def _():
            piece(b, y, at(x, y, z, 1 - core), 0).wait_recv()

        relay_sends(b, start)

    def sibling(b):
        return pltpu.make_async_remote_copy(src_ref=D.at[b], dst_ref=D.at[b], send_sem=ssend.at[b], recv_sem=srecv.at[b],
                                            device_id=at(x, y, z, 1 - core), device_id_type=MESH)

    def collect(b):
        cr = root(b)[2]

        @pl.when((core == cr) & has(b))
        def _():
            @pl.when(jnp.logical_not(on_root(b)))
            def _():
                for d in range(1, YS):
                    piece(b, lax.rem(y + d, YS), at(x, y, z, 1 - core), 0).wait_recv()
            sibling(b).start()

        @pl.when((core != cr) & has(b))
        def _():
            sibling(b).wait_recv()

    def drain(b):
        cr = root(b)[2]

        @pl.when(on_root(b) & (z >= (2 if b >= AJ0 else 0)))
        def _():
            scatter(b, finish)

        relay_sends(b, finish)

        @pl.when((core == cr) & has(b))
        def _():
            sibling(b).wait_send()

    def factor_tick(n):
        @pl.when(is_src)
        def _():
            @pl.when(n < 8)
            def _():
                factor_step(W, n)

            @pl.when(n == 8)
            def _():
                inv0 = W[:, NB:2 * NB]
                D[INV0] = inv0
                scatter(INV0, start)
                send_a10().wait_recv()
                send_a11().wait_recv()
                p10 = mm_nt(E[0], inv0)
                D[P10] = p10
                scatter(P10, start)
                factor_start(W, E[1] - mm_nt(p10, p10))

            @pl.when((n > 8) & (n < 17))
            def _():
                factor_step(W, n - 9)

            @pl.when(n == 17)
            def _():
                D[INV1] = W[:, NB:2 * NB]
                scatter(INV1, start)

    def tick(n, carry):
        ztick(n)
        factor_tick(n)
        return carry

    lax.fori_loop(0, CHUNKS + (ZS - 1) * SKEW, tick, 0)

    @pl.when(on_root(AJ0) & (z >= 2))
    def _():
        D[AJ0] = x0[0]
        D[AJ1] = x1[0]
        scatter(AJ0, start)
        scatter(AJ1, start)

    order = (INV0, P10, AJ0, AJ1, INV1)
    for b in order:
        relay(b)
    for b in order:
        collect(b)

    @pl.when(z == 0)
    def _():
        E[0] = D[INV0]

    @pl.when(z >= 1)
    def _():
        inv0, p10, inv1 = D[INV0], D[P10], D[INV1]

        @pl.when(z == 1)
        def _():
            E[1] = inv1
            E[0] = mm_nn(-mm_nn(inv1, p10), inv0)

        @pl.when(z >= 2)
        def _():
            pj0 = mm_nt(D[AJ0], inv0)
            pj1 = mm_nt(D[AJ1] - mm_nt(pj0, p10), inv1)
            t1 = -mm_nn(pj1, inv1)
            E[1] = t1
            E[0] = -mm_nn(pj0 + mm_nn(t1, p10), inv0)

    dn = (((1,), (1,)), ((), ()))
    for s in range(4):
        acc = jnp.where(z >= 2, a_ref[s].astype(F32), 0.0)
        xs = x0[s].astype(jnp.bfloat16)
        for t in split3(E[0])[::-1]:
            acc = acc + lax.dot_general(xs, t, dn, preferred_element_type=F32)
        o_ref[s] = acc

        @pl.when(z >= 1)
        def _():
            acc = o_ref[s]
            xs = x1[s].astype(jnp.bfloat16)
            for t in split3(E[1])[::-1]:
                acc = acc + lax.dot_general(xs, t, dn, preferred_element_type=F32)
            o_ref[s] = acc

    @pl.when(row <= z)
    def _():
        keep = row * NB + iota((NB, NB), 0) >= z * NB + iota((NB, NB), 1)
        o_ref[0] = jnp.where(keep, o_ref[0], 0.0)

    @pl.when(is_a10)
    def _():
        send_a10().wait_send()

    @pl.when(is_a11)
    def _():
        send_a11().wait_send()

    def zdrain(c, carry):
        for st in range(4):
            @pl.when(zsends(st))
            def _():
                zcopy(st, c).wait_send()
        return carry

    lax.fori_loop(0, CHUNKS, zdrain, 0)
    for b in order:
        drain(b)


def per_device(matrix):
    a = matrix.reshape(4, NB, NB)
    dma = pltpu.SemaphoreType.DMA
    out = pl.pallas_call(
        kernel,
        out_shape=jax.ShapeDtypeStruct((4, NB, NB), F32),
        in_specs=[pl.BlockSpec(memory_space=pltpu.VMEM)],
        out_specs=pl.BlockSpec(memory_space=pltpu.VMEM),
        scratch_shapes=[
            pltpu.VMEM((4, NB, NB), F32),
            pltpu.VMEM((4, NB, NB), F32),
            pltpu.VMEM((5, NB, NB), F32),
            pltpu.VMEM((2, NB, NB), F32),
            pltpu.VMEM((NB, 2 * NB), F32),
            dma((4, CHUNKS)), dma((4, CHUNKS)),
            dma((5, 24)), dma((5, YS)),
            dma((5,)), dma((5,)),
            dma((1,)), dma((2,)),
        ],
        compiler_params=pltpu.CompilerParams(collective_id=0, has_side_effects=True, vmem_limit_bytes=40 << 20),
    )(a)
    return out.reshape(4, NB, 1, NB)


def solution(mesh):
    return jax.shard_map(
        per_device,
        mesh=mesh,
        in_specs=(P(None, "row", None, "col"),),
        out_specs=P(None, "row", None, "col"),
        check_vma=False,
    )
```

time: 1070 us -> 86.7 us (0.08)
  the two profiles are of different devices: /device:TPU:1 before, /device:TPU:129 now
where the time goes in v1:
time: 86.7 us; the launch traced here: 86.5 us
  Pallas kernels  83.4 us (96%)
  local copies, waits for them, and re-layouts  3.09 us (4%)
    pallas_call x1, Pallas kernels, per_device(): pl.pallas_call(kernel, out_shape=jax.ShapeDtypeStruct((4, NB, NB), F32),...  83.4 us
    reshape x1, local copies, waits for them, and re-layouts, per_device(): return out.reshape(4, NB, 1, NB)  2.05 us

profile of v1, /device:TPU:129, one launch (start us, length us, event | category | flops | bytes accessed | tf_op | source)
XLA Modules:
  0.0 86.5 jit_solution(2776919047749244095)
XLA Ops:
  0.0 0.0 copy-start
  0.0 1.0 %copy-done = bf16[4,256,1,256]{3,1,2,0:T(8,128)(2,1)S(1)} copy-done((bf16[4,256,1,256]{3,1,2,0:T(8,128)(2,1)S(1)}, bf16[4,256,1,256]{3,1,2,0:T(8,128)(2,1)}, u32[]{:S(2)}) %copy-start) | copy-done | bytes 524312
  1.0 83.4 %shard_map.17 = f32[4,256,256]{2,1,0:T(8,128)S(1)} custom-call(bf16[4,256,256]{2,1,0:T(8,128)(2,1)S(1)} %bitcast.3), custom_call_target="tpu_custom_call" | custom-call | tf_op jit(solution)/shard_map/pallas_call | solution.py:429
  84.5 2.0 %copy.2 = f32[4,256,1,256]{3,2,1,0:T(1,128)} copy(f32[4,256,1,256]{3,1,0,2:T(8,128)S(1)} %bitcast.2) | data formatting | bytes 2097152 | tf_op jit(solution)/shard_map/reshape | solution.py:447
Async XLA Ops:
  0.0 1.0 %copy-start = (bf16[4,256,1,256]{3,1,2,0:T(8,128)(2,1)S(1)}, bf16[4,256,1,256]{3,1,2,0:T(8,128)(2,1)}, u32[]{:S(2)}) copy-start(bf16[4,256,1,256]{3,1,2,0:T(8,128)(2,1)} %param.1) | copy-start | bytes 1572868

commit v2 on v1

--- a/solution.py
+++ b/solution.py
@@ -11,11 +11,17 @@
 STEP = 32
 XS, YS, ZS = 4, 8, 8
 R = 32
-SKEW = 3
-PER = 128 // R
-CHUNKS = 4 * PER
+SKEW = 12
+UNITS = 4 * NB // R
+RING = 13
+COUNT = UNITS - RING
+EARLY = 4
+MID = 4
+TICKS = 40
 PIECE = NB // YS
 INV0, P10, INV1, AJ0, AJ1 = range(5)
+AT_INV0, AT_P10, AT_INV1, AT_AJ = 3, 9, 11, 6
+TO_X, TO_Z = 3, 4
 
 
 def split3(x):
@@ -101,7 +107,7 @@
         W[:, lo:lo + NB] = W[:, lo:lo + NB] - lax.dot_general(left, right, dn, preferred_element_type=F32)
 
 
-def kernel(a_ref, o_ref, x0, x1, D, E, W, zsend, zrecv, bsend, brecv, ssend, srecv, esend, erecv):
+def kernel(m_ref, o_ref, a_ref, x0, x1, D, E, W, asem, zsend, zrecv, bsend, brecv, ssend, srecv, esend, erecv):
     row = lax.axis_index("row")
     z = lax.axis_index("col")
     core = lax.rem(row, 2)
@@ -132,6 +138,23 @@
     def _():
         pl.semaphore_signal(barrier, inc=1, device_id=(0, 0), device_id_type=MESH)
 
+    hands = (row >= 2) & (row < ZS) & (z < 2)
+    line = (z >= 2) & (x == z // 2) & (core == lax.rem(z, 2)) & (y > 0)
+
+    @pl.when(hands)
+    def _():
+        for q in range(1, YS):
+            pl.semaphore_signal(barrier, inc=1, device_id=at(x, q, row, core), device_id_type=MESH)
+
+    @pl.when(line)
+    def _():
+        for p in range(2):
+            pl.semaphore_signal(barrier, inc=1, device_id=(z, p), device_id_type=MESH)
+
+    own = pltpu.make_async_copy(m_ref, a_ref, asem)
+    own.start()
+    own.wait()
+
     @pl.when(z == 0)
     def _():
         for s in range(4):
@@ -154,7 +177,14 @@
     def _():
         factor_start(W, x0[0])
 
-    pl.semaphore_wait(barrier, ZS + YS + XS - 2 + jnp.where(is_src | is_a11, 1, 0))
+        def step(k, carry):
+            factor_step(W, k)
+            return carry
+
+        lax.fori_loop(0, EARLY, step, 0)
+
+    peers = ZS + YS + XS - 2 + jnp.where(is_src | is_a11, 1, 0)
+    pl.semaphore_wait(barrier, peers + jnp.where(hands, YS - 1, 0) + jnp.where(line, 2, 0))
 
     def send_a10():
         return pltpu.make_async_remote_copy(src_ref=x0.at[0], dst_ref=E.at[0], send_sem=esend.at[0], recv_sem=erecv.at[0],
@@ -172,36 +202,77 @@
     def _():
         send_a11().start()
 
-    zp = lax.rem(z + 1, ZS)
-    zm = lax.rem(z + ZS - 1, ZS)
-    hops = (z, lax.rem(ZS - z, ZS), lax.rem(z + ZS - 1, ZS), lax.rem(ZS + 1 - z, ZS))
-    last = (ZS - 1, 1, ZS - 1, 2)
+    def hand(p, q):
+        rows = pl.ds(q * PIECE, PIECE)
+        return pltpu.make_async_remote_copy(src_ref=(x0, x1)[p].at[0, rows, :], dst_ref=D.at[AJ0 + p, rows, :],
+                                            send_sem=bsend.at[AJ0 + p, q], recv_sem=brecv.at[AJ0 + p, q],
+                                            device_id=at(x, q, row, core), device_id_type=MESH)
+
+    def hand_all(act):
+        for p in range(2):
+            @pl.when(hands & (z == p))
+            def _():
+                for q in range(YS):
+                    act(hand(p, q))
+
+    hand_all(lambda cp: cp.start())
+
+    hops = z, lax.rem(ZS - z, ZS), lax.rem(z + ZS - 1, ZS), lax.rem(ZS + 1 - z, ZS), z
+    up, down = lax.rem(z + 1, ZS), lax.rem(z + ZS - 1, ZS)
 
     def zcopy(st, c):
-        buf = x0 if st < 2 else x1
-        off = pl.multiple_of((0 if st % 2 == 0 else 128) + lax.rem(c, PER) * R, R)
-        ref = buf.at[c // PER, pl.ds(off, R), :]
+        buf = x0 if st < 2 or st == 4 else x1
+        odd = 0 if st in (0, 2) else 1
+        u = jnp.where(c < RING, 2 * c + odd, c + RING)
+        per = NB // R
+        ref = buf.at[u // per, pl.ds(pl.multiple_of(lax.rem(u, per) * R, R), R), :]
         return pltpu.make_async_remote_copy(src_ref=ref, dst_ref=ref, send_sem=zsend.at[st, c], recv_sem=zrecv.at[st, c],
-                                            device_id=(row, zp if st % 2 == 0 else zm), device_id_type=MESH)
-
-    def zreceives(st):
-        return (hops[st] > 0) & (z != 0) if st == 2 else hops[st] > 0
-
-    def zsends(st):
-        return (z != last[st]) & (z != 0) if st == 2 else z != last[st]
+                                            device_id=(row, down if st in (1, 3) else up), device_id_type=MESH)
+
+    def takes(st, c):
+        if st == 0:
+            return (z >= 1) & ((c < RING) | (z <= MID))
+        if st == 1:
+            return (z >= 2) & ((c < RING) | (z > MID))
+        if st == 2:
+            return (z >= 2) & ((c < RING) | (z <= MID))
+        if st == 3:
+            return (z != 1) & ((c < RING) | (z == 0) | (z > MID))
+        return (z == 1) & (c < RING)
+
+    def passes(st, c):
+        if st == 0:
+            return (z < ZS - 1) & ((c < RING) | (z < MID))
+        if st == 1:
+            return (z != 1) & (z != 2) & ((c < RING) | (z == 0) | (z > MID + 1))
+        if st == 2:
+            return (z >= 1) & (z < ZS - 1) & ((c < RING) | (z < MID))
+        if st == 3:
+            return (z != 2) & ((c < RING) | (z < 2) | (z > MID + 1))
+        return (z == 0) & (c < RING)
 
     def ztick(n):
-        for st in range(4):
-            c = n - hops[st] * SKEW
-            ok = (c >= 0) & (c < CHUNKS)
-
-            @pl.when(ok & zreceives(st))
+        for st in range(5):
+            c = n - (hops[st] * SKEW) // 4
+            ok = (c >= 0) & (c < COUNT)
+
+            @pl.when(ok & takes(st, c))
             def _():
                 zcopy(st, c).wait_recv()
 
-            @pl.when(ok & zsends(st))
-            def _():
-                zcopy(st, c).start()
+            if st in (0, 1, 4):
+                @pl.when(ok & passes(st, c) & jnp.logical_not(is_src))
+                def _():
+                    zcopy(st, c).start()
+
+                for c in (2 * n, 2 * n + 1):
+                    @pl.when(is_src & (c < COUNT) & passes(st, c))
+                    def _():
+                        zcopy(st, c).start()
+            else:
+                @pl.when(ok & passes(st, c))
+                def _():
+                    zcopy(st, c).start()
 
     def root(b):
         if b < AJ0:
@@ -218,7 +289,7 @@
 
     def on_root(b):
         xr, zr, cr = root(b)
-        return (x == xr) & (y == 0) & (z == zr) & (core == cr)
+        return (x == xr) & (y == 0) & (z == zr) & (core == cr) & (b < AJ0)
 
     def scatter(b, act):
         for d in range(1, YS):
@@ -226,20 +297,20 @@
 
     def send_x(b, act):
         for d in range(1, XS):
-            act(piece(b, y, at(lax.rem(x + d, XS), y, z, core), 6 + d))
+            act(piece(b, y, at(lax.rem(x + d, XS), y, z, core), 7 + d))
 
     def send_z(b, act):
         for d in range(1, ZS):
-            act(piece(b, y, at(x, y, d, core), 9 + d))
+            act(piece(b, y, at(x, y, d, core), 10 + d))
 
     def send_y(b, act):
         xr, zr, _ = root(b)
         for d in range(1, YS):
             to = lax.rem(y + d, YS)
 
-            @pl.when(jnp.logical_not((to == 0) & (x == xr) & (z == zr)))
-            def _():
-                act(piece(b, y, at(x, to, z, core), 16 + d))
+            @pl.when(jnp.logical_not((to == 0) & (x == xr) & (z == zr) & (b < AJ0)))
+            def _():
+                act(piece(b, y, at(x, to, z, core), 17 + d))
 
     def start(cp):
         cp.start()
@@ -247,39 +318,31 @@
     def finish(cp):
         cp.wait_send()
 
-    def relay_roles(b):
+    def relay_sends(b, act):
         xr, zr, cr = root(b)
         on_core = core == cr
-        first = on_core & (x == xr) & (z == zr)
-        second = on_core & (z == zr) if b < AJ0 else None
-        third = on_core & has(b)
-        return first, second, third
-
-    def relay_sends(b, act):
-        first, second, third = relay_roles(b)
-
-        @pl.when(first & (z >= (2 if b >= AJ0 else 0)))
+
+        @pl.when(on_core & (x == xr) & (z == zr) & (z >= (2 if b >= AJ0 else 0)))
         def _():
             send_x(b, act)
 
-        if second is not None:
-            @pl.when(second)
+        if b < AJ0:
+            @pl.when(on_core & (z == zr))
             def _():
                 send_z(b, act)
 
-        @pl.when(third)
+        @pl.when(on_core & has(b))
         def _():
             send_y(b, act)
 
     def relay(b):
         xr, zr, cr = root(b)
-        takes = (core == cr) & (has(b) | (z == zr)) if b < AJ0 else (core == cr) & has(b)
-
-        @pl.when(takes & jnp.logical_not(on_root(b)))
+        gets = (core == cr) & ((has(b) | (z == zr)) if b < AJ0 else has(b))
+
+        @pl.when(gets & jnp.logical_not(on_root(b)))
         def _():
             piece(b, y, at(x, y, z, 1 - core), 0).wait_recv()
-
-        relay_sends(b, start)
+            relay_sends(b, start)
 
     def sibling(b):
         return pltpu.make_async_remote_copy(src_ref=D.at[b], dst_ref=D.at[b], send_sem=ssend.at[b], recv_sem=srecv.at[b],
@@ -303,7 +366,7 @@
     def drain(b):
         cr = root(b)[2]
 
-        @pl.when(on_root(b) & (z >= (2 if b >= AJ0 else 0)))
+        @pl.when(on_root(b))
         def _():
             scatter(b, finish)
 
@@ -313,51 +376,71 @@
         def _():
             sibling(b).wait_send()
 
+    def stream(b, k):
+        rows = pl.ds(pl.multiple_of(k * PIECE, PIECE), PIECE)
+        D[b, rows, :] = W[rows, NB:2 * NB]
+
+        @pl.when(k > 0)
+        def _():
+            piece(b, k, at(x, k, z, core), k - 1).start()
+
+        @pl.when(k == 0)
+        def _():
+            relay_sends(b, start)
+
     def factor_tick(n):
-        @pl.when(is_src)
-        def _():
-            @pl.when(n < 8)
-            def _():
-                factor_step(W, n)
-
-            @pl.when(n == 8)
-            def _():
-                inv0 = W[:, NB:2 * NB]
-                D[INV0] = inv0
-                scatter(INV0, start)
-                send_a10().wait_recv()
-                send_a11().wait_recv()
-                p10 = mm_nt(E[0], inv0)
-                D[P10] = p10
-                scatter(P10, start)
-                factor_start(W, E[1] - mm_nt(p10, p10))
-
-            @pl.when((n > 8) & (n < 17))
-            def _():
-                factor_step(W, n - 9)
-
-            @pl.when(n == 17)
-            def _():
-                D[INV1] = W[:, NB:2 * NB]
-                scatter(INV1, start)
+        k = n + EARLY
+        at_p10 = NB // STEP
+
+        @pl.when(is_src & (k < at_p10))
+        def _():
+            factor_step(W, k)
+            stream(INV0, k)
+
+        @pl.when(is_src & (k == at_p10))
+        def _():
+            send_a10().wait_recv()
+            send_a11().wait_recv()
+            p10 = mm_nt(E[0], D[INV0])
+            D[P10] = p10
+            scatter(P10, start)
+            relay_sends(P10, start)
+            factor_start(W, E[1] - mm_nt(p10, p10))
+
+        @pl.when(is_src & (k > at_p10) & (k <= at_p10 + NB // STEP))
+        def _():
+            factor_step(W, k - at_p10 - 1)
+            stream(INV1, k - at_p10 - 1)
+
+    @pl.when(is_src)
+    def _():
+        def early(k, carry):
+            stream(INV0, k)
+            return carry
+
+        lax.fori_loop(0, EARLY, early, 0)
+
+    order = (INV0, P10, AJ0, AJ1, INV1)
+
+    def relay_at(b):
+        xr, zr, _ = root(b)
+        t = {INV0: AT_INV0 + jnp.maximum(y + 1 - EARLY, 0), P10: AT_P10, INV1: AT_INV1 + y, AJ0: AT_AJ, AJ1: AT_AJ}[b]
+        return t + jnp.where(x == xr, 0, TO_X) + (jnp.where(z == zr, 0, TO_Z) if b < AJ0 else 0)
+
+    when = [relay_at(b) for b in order]
 
     def tick(n, carry):
         ztick(n)
         factor_tick(n)
+
+        for b, t in zip(order, when):
+            @pl.when(n == t)
+            def _():
+                relay(b)
         return carry
 
-    lax.fori_loop(0, CHUNKS + (ZS - 1) * SKEW, tick, 0)
-
-    @pl.when(on_root(AJ0) & (z >= 2))
-    def _():
-        D[AJ0] = x0[0]
-        D[AJ1] = x1[0]
-        scatter(AJ0, start)
-        scatter(AJ1, start)
-
-    order = (INV0, P10, AJ0, AJ1, INV1)
-    for b in order:
-        relay(b)
+    lax.fori_loop(0, TICKS, tick, 0)
+
     for b in order:
         collect(b)
 
@@ -412,13 +495,15 @@
         send_a11().wait_send()
 
     def zdrain(c, carry):
-        for st in range(4):
-            @pl.when(zsends(st))
+        for st in range(5):
+            @pl.when(passes(st, c))
             def _():
                 zcopy(st, c).wait_send()
         return carry
 
-    lax.fori_loop(0, CHUNKS, zdrain, 0)
+    lax.fori_loop(0, COUNT, zdrain, 0)
+
+    hand_all(finish)
     for b in order:
         drain(b)
 
@@ -429,16 +514,17 @@
     out = pl.pallas_call(
         kernel,
         out_shape=jax.ShapeDtypeStruct((4, NB, NB), F32),
-        in_specs=[pl.BlockSpec(memory_space=pltpu.VMEM)],
+        in_specs=[pl.BlockSpec(memory_space=pl.ANY)],
         out_specs=pl.BlockSpec(memory_space=pltpu.VMEM),
         scratch_shapes=[
+            pltpu.VMEM((4, NB, NB), jnp.bfloat16),
             pltpu.VMEM((4, NB, NB), F32),
             pltpu.VMEM((4, NB, NB), F32),
             pltpu.VMEM((5, NB, NB), F32),
             pltpu.VMEM((2, NB, NB), F32),
             pltpu.VMEM((NB, 2 * NB), F32),
-            dma((4, CHUNKS)), dma((4, CHUNKS)),
-            dma((5, 24)), dma((5, YS)),
+            dma(()), dma((5, COUNT)), dma((5, COUNT)),
+            dma((5, 25)), dma((5, YS)),
             dma((5,)), dma((5,)),
             dma((1,)), dma((2,)),
         ],

time: 86.7 us -> 73.6 us (0.85)
  the two profiles are of different devices: /device:TPU:129 before, /device:TPU:135 now
where the time goes in v2:
time: 73.6 us; the launch traced here: 73.4 us
  Pallas kernels  70.3 us (96%)
  local copies, waits for them, and re-layouts  3.09 us (4%)
    pallas_call x1, Pallas kernels, per_device(): pl.pallas_call(kernel, out_shape=jax.ShapeDtypeStruct((4, NB, NB), F32),...  70.3 us
    reshape x1, local copies, waits for them, and re-layouts, per_device(): return out.reshape(4, NB, 1, NB)  2.05 us

profile of v2, /device:TPU:135, one launch (start us, length us, event | category | flops | bytes accessed | tf_op | source)
XLA Modules:
  0.0 73.4 jit_solution(10180353426677197308)
XLA Ops:
  0.0 0.0 copy-start
  0.0 1.0 %copy-done = bf16[4,256,1,256]{3,1,2,0:T(8,128)(2,1)S(1)} copy-done((bf16[4,256,1,256]{3,1,2,0:T(8,128)(2,1)S(1)}, bf16[4,256,1,256]{3,1,2,0:T(8,128)(2,1)}, u32[]{:S(2)}) %copy-start) | copy-done | bytes 524312
  1.0 70.3 %shard_map.17 = f32[4,256,256]{2,1,0:T(8,128)S(1)} custom-call(bf16[4,256,256]{2,1,0:T(8,128)(2,1)S(1)} %bitcast.3), custom_call_target="tpu_custom_call" | custom-call | tf_op jit(solution)/shard_map/pallas_call | solution.py:514
  71.4 2.0 %copy.2 = f32[4,256,1,256]{3,2,1,0:T(1,128)} copy(f32[4,256,1,256]{3,1,0,2:T(8,128)S(1)} %bitcast.2) | data formatting | bytes 2097152 | tf_op jit(solution)/shard_map/reshape | solution.py:533
Async XLA Ops:
  0.0 1.0 %copy-start = (bf16[4,256,1,256]{3,1,2,0:T(8,128)(2,1)S(1)}, bf16[4,256,1,256]{3,1,2,0:T(8,128)(2,1)}, u32[]{:S(2)}) copy-start(bf16[4,256,1,256]{3,1,2,0:T(8,128)(2,1)} %param.1) | copy-start | bytes 1572868

commit v3 on v2

--- a/solution.py
+++ b/solution.py
@@ -20,7 +20,7 @@
 TICKS = 40
 PIECE = NB // YS
 INV0, P10, INV1, AJ0, AJ1 = range(5)
-AT_INV0, AT_P10, AT_INV1, AT_AJ = 3, 9, 11, 6
+AT_INV0, AT_P10, AT_INV1, AT_AJ, AT_HAND = 3, 9, 11, 9, 4
 TO_X, TO_Z = 3, 4
 
 
@@ -107,7 +107,7 @@
         W[:, lo:lo + NB] = W[:, lo:lo + NB] - lax.dot_general(left, right, dn, preferred_element_type=F32)
 
 
-def kernel(m_ref, o_ref, a_ref, x0, x1, D, E, W, asem, zsend, zrecv, bsend, brecv, ssend, srecv, esend, erecv):
+def kernel(m_ref, o_ref, a_ref, x0, x1, D, E, W, via, asem, zsend, zrecv, vsend, vrecv, gsend, grecv, bsend, brecv, ssend, srecv, esend, erecv):
     row = lax.axis_index("row")
     z = lax.axis_index("col")
     core = lax.rem(row, 2)
@@ -130,6 +130,9 @@
         pl.semaphore_signal(barrier, inc=1, device_id=at(lax.rem(x + d, XS), y, z, core), device_id_type=MESH)
     pl.semaphore_signal(barrier, inc=1, device_id=at(x, y, z, 1 - core), device_id_type=MESH)
 
+    for d in (1, ZS - 1):
+        pl.semaphore_signal(barrier, inc=1, device_id=at(x, y, lax.rem(z + d, ZS), 1 - core), device_id_type=MESH)
+
     @pl.when(is_src)
     def _():
         pl.semaphore_signal(barrier, inc=1, device_id=(1, 1), device_id_type=MESH)
@@ -137,23 +140,13 @@
     @pl.when(is_a11)
     def _():
         pl.semaphore_signal(barrier, inc=1, device_id=(0, 0), device_id_type=MESH)
-
-    hands = (row >= 2) & (row < ZS) & (z < 2)
-    line = (z >= 2) & (x == z // 2) & (core == lax.rem(z, 2)) & (y > 0)
-
-    @pl.when(hands)
-    def _():
-        for q in range(1, YS):
-            pl.semaphore_signal(barrier, inc=1, device_id=at(x, q, row, core), device_id_type=MESH)
-
-    @pl.when(line)
-    def _():
-        for p in range(2):
-            pl.semaphore_signal(barrier, inc=1, device_id=(z, p), device_id_type=MESH)
 
     own = pltpu.make_async_copy(m_ref, a_ref, asem)
     own.start()
-    own.wait()
+
+    @pl.when(z < 2)
+    def _():
+        own.wait()
 
     @pl.when(z == 0)
     def _():
@@ -183,8 +176,7 @@
 
         lax.fori_loop(0, EARLY, step, 0)
 
-    peers = ZS + YS + XS - 2 + jnp.where(is_src | is_a11, 1, 0)
-    pl.semaphore_wait(barrier, peers + jnp.where(hands, YS - 1, 0) + jnp.where(line, 2, 0))
+    pl.semaphore_wait(barrier, ZS + YS + XS + jnp.where(is_src | is_a11, 1, 0))
 
     def send_a10():
         return pltpu.make_async_remote_copy(src_ref=x0.at[0], dst_ref=E.at[0], send_sem=esend.at[0], recv_sem=erecv.at[0],
@@ -201,33 +193,77 @@
     @pl.when(is_a11)
     def _():
         send_a11().start()
+
+    goal = 2 * x + core
 
     def hand(p, q):
         rows = pl.ds(q * PIECE, PIECE)
         return pltpu.make_async_remote_copy(src_ref=(x0, x1)[p].at[0, rows, :], dst_ref=D.at[AJ0 + p, rows, :],
                                             send_sem=bsend.at[AJ0 + p, q], recv_sem=brecv.at[AJ0 + p, q],
-                                            device_id=at(x, q, row, core), device_id_type=MESH)
-
-    def hand_all(act):
+                                            device_id=at(x, q, z, core), device_id_type=MESH)
+
+    def hand_first(p):
+        rows = pl.ds(0, PIECE)
+        return pltpu.make_async_remote_copy(src_ref=(x0, x1)[p].at[0, rows, :], dst_ref=D.at[AJ0 + p, rows, :],
+                                            send_sem=bsend.at[AJ0 + p, 0], recv_sem=brecv.at[AJ0 + p, 0],
+                                            device_id=at(x, y, goal, core), device_id_type=MESH)
+
+    def hand_on(p):
+        ref = D.at[AJ0 + p, pl.ds(pl.multiple_of(y * PIECE, PIECE), PIECE), :]
+        return pltpu.make_async_remote_copy(src_ref=ref, dst_ref=ref, send_sem=bsend.at[AJ0 + p, 0], recv_sem=brecv.at[AJ0 + p, y],
+                                            device_id=at(x, y, goal, core), device_id_type=MESH)
+
+    def hand_out(act):
         for p in range(2):
-            @pl.when(hands & (z == p))
-            def _():
-                for q in range(YS):
+            @pl.when((z == p) & (goal >= 2) & (y == 0))
+            def _():
+                act(hand_first(p))
+                for q in range(1, YS):
                     act(hand(p, q))
 
-    hand_all(lambda cp: cp.start())
+    def hand_over(act):
+        for p in range(2):
+            @pl.when((z == p) & (goal >= 2) & (y > 0))
+            def _():
+                act(p)
+
+    def pass_on(p):
+        hand_on(p).wait_recv()
+        hand_on(p).start()
+
+    hand_out(lambda cp: cp.start())
 
     hops = z, lax.rem(ZS - z, ZS), lax.rem(z + ZS - 1, ZS), lax.rem(ZS + 1 - z, ZS), z
     up, down = lax.rem(z + 1, ZS), lax.rem(z + ZS - 1, ZS)
-
-    def zcopy(st, c):
+    other = at(x, y, z, 1 - core)
+
+    def place(st, c):
         buf = x0 if st < 2 or st == 4 else x1
         odd = 0 if st in (0, 2) else 1
         u = jnp.where(c < RING, 2 * c + odd, c + RING)
         per = NB // R
-        ref = buf.at[u // per, pl.ds(pl.multiple_of(lax.rem(u, per) * R, R), R), :]
+        return buf.at[u // per, pl.ds(pl.multiple_of(lax.rem(u, per) * R, R), R), :]
+
+    def to(st, core_):
+        return at(x, y, down if st in (1, 3) else up, core_)
+
+    def zcopy(st, c):
+        ref = place(st, c)
         return pltpu.make_async_remote_copy(src_ref=ref, dst_ref=ref, send_sem=zsend.at[st, c], recv_sem=zrecv.at[st, c],
-                                            device_id=(row, down if st in (1, 3) else up), device_id_type=MESH)
+                                            device_id=to(st, core), device_id_type=MESH)
+
+    def enter(st, c):
+        return pltpu.make_async_remote_copy(src_ref=place(st, c), dst_ref=via.at[st // 2, c], send_sem=zsend.at[st, c],
+                                            recv_sem=vrecv.at[st // 2, c], device_id=to(st, 1 - core), device_id_type=MESH)
+
+    def vcopy(st, c):
+        ref = via.at[st // 2, c]
+        return pltpu.make_async_remote_copy(src_ref=ref, dst_ref=ref, send_sem=vsend.at[st // 2, c], recv_sem=vrecv.at[st // 2, c],
+                                            device_id=to(st, core), device_id_type=MESH)
+
+    def give(st, c):
+        return pltpu.make_async_remote_copy(src_ref=via.at[st // 2, c], dst_ref=place(st, c), send_sem=gsend.at[st // 2, c],
+                                            recv_sem=grecv.at[st // 2, c], device_id=other, device_id_type=MESH)
 
     def takes(st, c):
         if st == 0:
@@ -251,28 +287,62 @@
             return (z != 2) & ((c < RING) | (z < 2) | (z > MID + 1))
         return (z == 0) & (c < RING)
 
+    def on_lane(st):
+        return core == st % 2
+
+    def begins(st):
+        return z == st // 2
+
+    def keeps(st):
+        return z != 0
+
     def ztick(n):
-        for st in range(5):
+        for st in range(4):
             c = n - (hops[st] * SKEW) // 4
             ok = (c >= 0) & (c < COUNT)
 
-            @pl.when(ok & takes(st, c))
-            def _():
-                zcopy(st, c).wait_recv()
-
-            if st in (0, 1, 4):
-                @pl.when(ok & passes(st, c) & jnp.logical_not(is_src))
+            @pl.when(ok & on_lane(st))
+            def _():
+                @pl.when(takes(st, c))
+                def _():
+                    zcopy(st, c).wait_recv()
+
+                @pl.when(passes(st, c))
                 def _():
                     zcopy(st, c).start()
 
-                for c in (2 * n, 2 * n + 1):
-                    @pl.when(is_src & (c < COUNT) & passes(st, c))
+                @pl.when(takes(st, c))
+                def _():
+                    vcopy(st, c).wait_recv()
+
+                    @pl.when(passes(st, c))
                     def _():
-                        zcopy(st, c).start()
-            else:
-                @pl.when(ok & passes(st, c))
-                def _():
-                    zcopy(st, c).start()
+                        vcopy(st, c).start()
+
+                    @pl.when(keeps(st))
+                    def _():
+                        give(st, c).start()
+
+            @pl.when(ok & jnp.logical_not(on_lane(st)) & begins(st))
+            def _():
+                enter(st, c).start()
+
+        c = n - (hops[4] * SKEW) // 4
+
+        @pl.when((c >= 0) & (c < COUNT) & passes(4, c))
+        def _():
+            zcopy(4, c).start()
+
+    def zfinish(c, carry):
+        @pl.when(takes(4, c))
+        def _():
+            zcopy(4, c).wait_recv()
+
+        for st in range(4):
+            @pl.when(jnp.logical_not(on_lane(st)) & takes(st, c) & keeps(st))
+            def _():
+                give(st, c).wait_recv()
+        return carry
 
     def root(b):
         if b < AJ0:
@@ -433,6 +503,10 @@
         ztick(n)
         factor_tick(n)
 
+        @pl.when(n == AT_HAND)
+        def _():
+            hand_over(pass_on)
+
         for b, t in zip(order, when):
             @pl.when(n == t)
             def _():
@@ -440,13 +514,19 @@
         return carry
 
     lax.fori_loop(0, TICKS, tick, 0)
+    lax.fori_loop(0, COUNT, zfinish, 0)
 
     for b in order:
         collect(b)
 
+    @pl.when(z >= 2)
+    def _():
+        own.wait()
+
     @pl.when(z == 0)
     def _():
         E[0] = D[INV0]
+        E[1] = jnp.zeros((NB, NB), F32)
 
     @pl.when(z >= 1)
     def _():
@@ -466,25 +546,20 @@
             E[0] = -mm_nn(pj0 + mm_nn(t1, p10), inv0)
 
     dn = (((1,), (1,)), ((), ()))
+    t0 = split3(E[0])[::-1]
+    t1 = split3(E[1])[::-1]
     for s in range(4):
         acc = jnp.where(z >= 2, a_ref[s].astype(F32), 0.0)
         xs = x0[s].astype(jnp.bfloat16)
-        for t in split3(E[0])[::-1]:
+        for t in t0:
             acc = acc + lax.dot_general(xs, t, dn, preferred_element_type=F32)
-        o_ref[s] = acc
-
-        @pl.when(z >= 1)
-        def _():
-            acc = o_ref[s]
-            xs = x1[s].astype(jnp.bfloat16)
-            for t in split3(E[1])[::-1]:
-                acc = acc + lax.dot_general(xs, t, dn, preferred_element_type=F32)
-            o_ref[s] = acc
-
-    @pl.when(row <= z)
-    def _():
-        keep = row * NB + iota((NB, NB), 0) >= z * NB + iota((NB, NB), 1)
-        o_ref[0] = jnp.where(keep, o_ref[0], 0.0)
+        xs = jnp.where(z >= 1, x1[s], 0.0).astype(jnp.bfloat16)
+        for t in t1:
+            acc = acc + lax.dot_general(xs, t, dn, preferred_element_type=F32)
+        if s == 0:
+            acc = jnp.where((row > z) | (row * NB + iota((NB, NB), 0) >= z * NB + iota((NB, NB), 1)), acc, 0.0)
+        for h in range(2):
+            o_ref[pl.ds(2 * NB * s + h, NB, stride=2), :] = acc[:, 128 * h:128 * h + 128]
 
     @pl.when(is_a10)
     def _():
@@ -495,15 +570,34 @@
         send_a11().wait_send()
 
     def zdrain(c, carry):
-        for st in range(5):
-            @pl.when(passes(st, c))
+        for st in range(4):
+            @pl.when(on_lane(st) & passes(st, c))
             def _():
                 zcopy(st, c).wait_send()
+
+            @pl.when(on_lane(st) & takes(st, c))
+            def _():
+                @pl.when(passes(st, c))
+                def _():
+                    vcopy(st, c).wait_send()
+
+                @pl.when(keeps(st))
+                def _():
+                    give(st, c).wait_send()
+
+            @pl.when(jnp.logical_not(on_lane(st)) & begins(st))
+            def _():
+                enter(st, c).wait_send()
+
+        @pl.when(passes(4, c))
+        def _():
+            zcopy(4, c).wait_send()
         return carry
 
     lax.fori_loop(0, COUNT, zdrain, 0)
 
-    hand_all(finish)
+    hand_out(finish)
+    hand_over(lambda p: hand_on(p).wait_send())
     for b in order:
         drain(b)
 
@@ -513,8 +607,8 @@
     dma = pltpu.SemaphoreType.DMA
     out = pl.pallas_call(
         kernel,
-        out_shape=jax.ShapeDtypeStruct((4, NB, NB), F32),
-        in_specs=[pl.BlockSpec(memory_space=pl.ANY)],
+        out_shape=jax.ShapeDtypeStruct((8 * NB, 128), F32),
+        in_specs=[pl.BlockSpec(memory_space=pltpu.HBM)],
         out_specs=pl.BlockSpec(memory_space=pltpu.VMEM),
         scratch_shapes=[
             pltpu.VMEM((4, NB, NB), jnp.bfloat16),
@@ -523,7 +617,9 @@
             pltpu.VMEM((5, NB, NB), F32),
             pltpu.VMEM((2, NB, NB), F32),
             pltpu.VMEM((NB, 2 * NB), F32),
+            pltpu.VMEM((2, COUNT, R, NB), F32),
             dma(()), dma((5, COUNT)), dma((5, COUNT)),
+            dma((2, COUNT)), dma((2, COUNT)), dma((2, COUNT)), dma((2, COUNT)),
             dma((5, 25)), dma((5, YS)),
             dma((5,)), dma((5,)),
             dma((1,)), dma((2,)),

time: 73.6 us -> 66.2 us (0.90)
  the two profiles are of different devices: /device:TPU:135 before, /device:TPU:449 now
where the time goes in v3:
time: 66.2 us; the launch traced here: 66 us
  Pallas kernels  64 us (97%)
  local copies, waits for them, and re-layouts  2.01 us (3%)
    pallas_call x1, Pallas kernels, per_device(): pl.pallas_call(kernel, out_shape=jax.ShapeDtypeStruct((8 * NB, 128), F32)...  64 us
    unnamed x3, local copies, waits for them, and re-layouts  2.01 us

profile of v3, /device:TPU:449, one launch (start us, length us, event | category | flops | bytes accessed | tf_op | source)
XLA Modules:
  0.0 66.0 jit_solution(4460974269088512532)
XLA Ops:
  0.0 0.0 copy-start
  0.0 1.0 %copy-done = bf16[4,256,1,256]{3,1,2,0:T(8,128)(2,1)S(1)} copy-done((bf16[4,256,1,256]{3,1,2,0:T(8,128)(2,1)S(1)}, bf16[4,256,1,256]{3,1,2,0:T(8,128)(2,1)}, u32[]{:S(2)}) %copy-start) | copy-done | bytes 524312
  1.0 64.0 %shard_map.17 = f32[2048,128]{1,0:T(8,128)S(1)} custom-call(bf16[4,256,256]{2,1,0:T(8,128)(2,1)S(1)} %bitcast.3), custom_call_target="tpu_custom_call" | custom-call | tf_op jit(solution)/shard_map/pallas_call | solution.py:608
  65.0 1.0 %copy.4 = f32[4,256,1,256]{3,2,1,0:T(1,128)} copy(f32[4,256,1,256]{3,2,1,0:T(1,128)S(1)} %bitcast.2) | data formatting | bytes 2097152
Async XLA Ops:
  0.0 1.0 %copy-start = (bf16[4,256,1,256]{3,1,2,0:T(8,128)(2,1)S(1)}, bf16[4,256,1,256]{3,1,2,0:T(8,128)(2,1)}, u32[]{:S(2)}) copy-start(bf16[4,256,1,256]{3,1,2,0:T(8,128)(2,1)} %param.1) | copy-start | bytes 1572868

commit v4 on v3

--- a/solution.py
+++ b/solution.py
@@ -327,7 +327,7 @@
             def _():
                 enter(st, c).start()
 
-        c = n - (hops[4] * SKEW) // 4
+        c = n - COUNT
 
         @pl.when((c >= 0) & (c < COUNT) & passes(4, c))
         def _():

time: 66.2 us -> 65.9 us (level)
  the two profiles are of different devices: /device:TPU:449 before, /device:TPU:129 now
where the time goes in v4:
time: 65.9 us; the launch traced here: 65.8 us
  Pallas kernels  63.8 us (97%)
  local copies, waits for them, and re-layouts  2.01 us (3%)
    pallas_call x1, Pallas kernels, per_device(): pl.pallas_call(kernel, out_shape=jax.ShapeDtypeStruct((8 * NB, 128), F32)...  63.8 us
    unnamed x3, local copies, waits for them, and re-layouts  2.01 us

profile of v4, /device:TPU:129, one launch (start us, length us, event | category | flops | bytes accessed | tf_op | source)
XLA Modules:
  0.0 65.8 jit_solution(5701738830400595064)
XLA Ops:
  0.0 0.0 copy-start
  0.0 1.0 %copy-done = bf16[4,256,1,256]{3,1,2,0:T(8,128)(2,1)S(1)} copy-done((bf16[4,256,1,256]{3,1,2,0:T(8,128)(2,1)S(1)}, bf16[4,256,1,256]{3,1,2,0:T(8,128)(2,1)}, u32[]{:S(2)}) %copy-start) | copy-done | bytes 524312
  1.0 63.8 %shard_map.17 = f32[2048,128]{1,0:T(8,128)S(1)} custom-call(bf16[4,256,256]{2,1,0:T(8,128)(2,1)S(1)} %bitcast.3), custom_call_target="tpu_custom_call" | custom-call | tf_op jit(solution)/shard_map/pallas_call | solution.py:608
  64.8 1.0 %copy.4 = f32[4,256,1,256]{3,2,1,0:T(1,128)} copy(f32[4,256,1,256]{3,2,1,0:T(1,128)S(1)} %bitcast.2) | data formatting | bytes 2097152
Async XLA Ops:
  0.0 1.0 %copy-start = (bf16[4,256,1,256]{3,1,2,0:T(8,128)(2,1)S(1)}, bf16[4,256,1,256]{3,1,2,0:T(8,128)(2,1)}, u32[]{:S(2)}) copy-start(bf16[4,256,1,256]{3,1,2,0:T(8,128)(2,1)} %param.1) | copy-start | bytes 1572868
